TPU v7x, 128 devices: a whole 4x4x4 slice. The times are simulated.
128 devices in a mesh: str: 16 (over x_lo, y, core), crs: 8 (over x_hi, z).
Axes of the slice: x: 4 (x_hi: 2, x_lo: 2; x = x_hi * 2 + x_lo), y: 4, z: 4, core: 2. Of those that a mesh axis runs over, the one named last changes fastest.
Arguments:
- voltage: float32 [4, 512, 16384], P(None, 'str', 'crs'), may hold values from -4 to 0.5
- photocurrent: float32 [4, 512, 16384], P(None, 'str', 'crs'), may hold values from 0.1 to 10
- shunt: float32 [512, 16384], P('str', 'crs'), may hold values from 0.02 to 0.5
- series: float32 [512, 16384], P('str', 'crs'), may hold values from 0.5 to 2
- pattern: int32 [512, 128], P('str', 'crs'), may hold values from 0 to 3
- diode_mask: int32 [512, 128], P('str', 'crs'), may hold values 0 or 1
- aggregate: int32 [512, 128], P('str', 'crs'), may hold values from 0 to 4095, as said below
- coarse_inverse: float32 [4096, 4096], P('crs'), as said below
Outputs:
- newton_step: float32 [4, 512, 16384], P(None, 'str', 'crs')
- residual: float32 [4, 512, 16384], P(None, 'str', 'crs')
Inputs may be any that keep to these rules, and one draw needn't show every extreme that they name: `aggregate`: every value appears. coarse_inverse is symmetric positive definite.
All inputs are finite; a program needn't handle non-finite values. No bound on the sum of `diode_mask` on one device may be relied on, other than what follows from the above.
Results may differ from a plain program's by a relative error of at most 0.0003.
Values sent between devices are 32-bit elements; how exact they have to be, the bound alone decides.
A program may use at most 64 MiB of HBM per device.

v0:
```python
import jax
import jax.numpy as jnp
from jax import lax
from jax.sharding import PartitionSpec as P

ITERS = 3
LEVELS = (0.25, 0.5, 1.0, 2.0)
DIODE_SAT = 0.5


def with_halo(block, sides, width, periodic):
    for axis, dim in sides:
        count = lax.axis_size(axis)
        forward = [(i, i + 1) for i in range(count - 1)]
        if periodic:
            forward.append((count - 1, 0))
        backward = [(target, source) for source, target in forward]
        low = lax.ppermute(
            lax.slice_in_dim(block, block.shape[dim] - width, None, axis=dim), axis, forward
        )
        high = lax.ppermute(lax.slice_in_dim(block, 0, width, axis=dim), axis, backward)
        block = jnp.concatenate([low, block, high], axis=dim)
    return block


def widen(blocks):
    shape = blocks.shape
    spread = jnp.broadcast_to(blocks[..., None], shape + (128,))
    return spread.reshape(shape[:-1] + (shape[-1] * 128,))


def cross_levels(pattern):
    total = jnp.zeros(pattern.shape, jnp.float32)
    for number in range(4):
        total = total + jnp.where(pattern == number, jnp.float32(LEVELS[number]), jnp.float32(0.0))
    return total


def neighbours(field):
    along = with_halo(field, (("str", 1),), 1, True)
    across = with_halo(field, (("crs", 2),), 1, False)
    return (along[:, 2:], along[:, :-2], across[:, :, 2:], across[:, :, :-2])


def shards(voltage, photocurrent, shunt, series, pattern, diode_mask, aggregate, coarse_inverse):
    points = voltage.shape[0]
    rows_here = voltage.shape[1]
    local_block_list = voltage.shape[2] // 128
    coarse_count = coarse_inverse.shape[1]
    cross_level = widen(cross_levels(pattern))
    diode_area = widen(diode_mask.astype(jnp.float32))
    flat_groups = aggregate.reshape(-1)
    stacked = jnp.concatenate([voltage, cross_level[None], series[None]], axis=0)
    below, above, right_cells, left_cells = neighbours(stacked)
    right_link = jnp.minimum(cross_level, right_cells[points])
    left_link = jnp.minimum(cross_level, left_cells[points])
    up_link = above[points + 1]
    diode_derivative = DIODE_SAT * diode_area * jnp.exp(voltage)
    imbalance = (
        shunt * voltage
        + series * (voltage - below[:points])
        + up_link * (voltage - above[:points])
        + right_link * (voltage - right_cells[:points])
        + left_link * (voltage - left_cells[:points])
        + diode_derivative
        - DIODE_SAT * diode_area
        - photocurrent
    )
    diagonal = shunt + diode_derivative + series + up_link + right_link + left_link

    def restrict(remainder):
        block_sums = remainder.reshape(points, rows_here * local_block_list, 128).sum(axis=-1)
        return jax.ops.segment_sum(block_sums.T, flat_groups, num_segments=coarse_count).T

    def interpolate_upward(correction):
        picked = jnp.take(correction, flat_groups, axis=1)
        return widen(picked.reshape(points, rows_here, local_block_list))

    def coarse_solve(incomplete_value):
        product = None
        total = lax.psum(incomplete_value, ("str", "crs"))
        row_share = lax.dot_general(
            total, coarse_inverse, (((1,), (1,)), ((), ())), precision=lax.Precision.HIGHEST
        )
        correction = lax.all_gather(row_share, "crs", axis=1, tiled=True)
        return (correction, product)

    def precondition(remainder):
        resident_portion = remainder / diagonal
        incomplete_value = restrict(remainder)
        correction, product = coarse_solve(incomplete_value)
        smoothed = resident_portion + interpolate_upward(correction)
        product = lax.psum(jnp.sum(remainder * smoothed, axis=(1, 2)), ("str", "crs"))
        return (smoothed, product)

    remainder = -imbalance
    newton_step = jnp.zeros_like(voltage)
    smoothed, product = precondition(remainder)
    direction = smoothed
    for turn in range(ITERS):
        operate_below, operate_above, operate_right_cells, operate_left_cells = neighbours(
            direction
        )
        image = (
            diagonal * direction
            - series * operate_below
            - up_link * operate_above
            - right_link * operate_right_cells
            - left_link * operate_left_cells
        )
        curvature = lax.psum(jnp.sum(direction * image, axis=(1, 2)), ("str", "crs"))
        alpha = (product / curvature)[:, None, None]
        newton_step = newton_step + alpha * direction
        remainder = remainder - alpha * image
        if turn + 1 < ITERS:
            smoothed, fresh = precondition(remainder)
            ratio = (fresh / product)[:, None, None]
            direction = smoothed + ratio * direction
            product = fresh
    return (newton_step, remainder)


def solution(mesh):
    placed = (
        P(None, "str", "crs"),
        P(None, "str", "crs"),
        P("str", "crs"),
        P("str", "crs"),
        P("str", "crs"),
        P("str", "crs"),
        P("str", "crs"),
        P("crs", None),
    )
    return jax.shard_map(
        shards,
        mesh=mesh,
        in_specs=placed,
        out_specs=(P(None, "str", "crs"), P(None, "str", "crs")),
        check_vma=False,
    )
```

profile of v0, /device:TPU:1, one launch (start us, length us, event | category | flops | bytes accessed | tf_op | source)
XLA Modules:
  0.0 1062.8 jit_solution(3380685636923150555)
XLA Ops:
  13.7 4.2 collective-permute-start.3
  26.5 3.8 scatter_custom_fusion
  30.4 158.7 %all-reduce.5.cloned.1.call-done = f32[4,4096]{0,1:T(8,128)} async-done(((f32[4,4096]{0,1:T(8,128)}), f32[4,4096]{0,1:T(8,128)}) %all-reduce.5.cloned.1.call-update) | async-done | bytes 65552 | tf_op jit(solution)/shard_map/psum | solution.py:81
  189.0 10.9 %fusion.54 = f32[4,512]{1,0:T(4,128)S(1)} fusion(f32[4,4096]{0,1:T(8,128)} %all-reduce.5.cloned.1.call-done, f32[512,4096]{1,0:T(8,128)} %param.17), kind=kOutput, calls=%fused_computation.118 | convolution fusion | flops 100663296 | bytes 8462336 | tf_op jit(solution)/shard_map/dot_general | solution.py:82
  199.9 28.1 %all_gather.9 = f32[4,4096]{1,0:T(4,128)S(1)} all-gather(f32[4,512]{1,0:T(4,128)S(1)} %fusion.54), channel_id=1, replica_groups=mesh['str'=16,'crs'=8] {'crs'}, dimensions={1}, use_global_device_ids=true | all-gather | bytes 73728 | tf_op jit(solution)/shard_map/all_gather | solution.py:85
  235.8 7.2 collective-permute-start.4
  245.6 4.0 collective-permute-start.7
  252.5 69.2 %all-reduce = (f32[4]{0:T(128)}, f32[4]{0:T(128)}) all-reduce(f32[4]{0:T(128)S(1)} %get-tuple-element.4, f32[4]{0:T(128)S(1)} %get-tuple-element.3), channel_id=1, replica_groups=mesh['str'=16,'crs'=8] {'str','crs'}, use_global_device_ids=true, to_apply=%region_4.6 | all-reduce | flops 8 | bytes 64 | tf_op jit(solution)/shard_map/psum | solution.py:93
  327.1 3.8 scatter_custom_fusion.1
  331.1 147.5 %all-reduce.7.cloned.1.call-done = f32[4,4096]{0,1:T(8,128)} async-done(((f32[4,4096]{0,1:T(8,128)}), f32[4,4096]{0,1:T(8,128)}) %all-reduce.7.cloned.1.call-update) | async-done | bytes 65552 | tf_op jit(solution)/shard_map/psum | solution.py:81
  478.6 10.9 %fusion.55 = f32[4,512]{1,0:T(4,128)S(1)} fusion(f32[4,4096]{0,1:T(8,128)} %all-reduce.7.cloned.1.call-done, f32[512,4096]{1,0:T(8,128)} %param.17), kind=kOutput, calls=%fused_computation.119 | convolution fusion | flops 100663296 | bytes 8462336 | tf_op jit(solution)/shard_map/dot_general | solution.py:82
  489.4 27.8 %all_gather.10 = f32[4,4096]{1,0:T(4,128)S(1)} all-gather(f32[4,512]{1,0:T(4,128)S(1)} %fusion.55), channel_id=1, replica_groups=mesh['str'=16,'crs'=8] {'crs'}, dimensions={1}, use_global_device_ids=true | all-gather | bytes 73728 | tf_op jit(solution)/shard_map/all_gather | solution.py:85
  519.2 3.3 gather_fusion.1
  530.8 70.0 %psum.67 = f32[4]{0:T(128)S(1)} all-reduce(f32[4]{0:T(128)S(1)} %multiply_reduce_fusion.3), channel_id=1, replica_groups=mesh['str'=16,'crs'=8] {'str','crs'}, use_global_device_ids=true, to_apply=%region_11.13 | all-reduce | flops 4 | bytes 32 | tf_op jit(solution)/shard_map/psum | solution.py:93
  606.0 4.0 collective-permute-start.11
  613.3 71.4 %psum.68 = f32[4]{0:T(128)} all-reduce(f32[4]{0:T(128)S(1)} %multiply_reduce_fusion.2), channel_id=1, replica_groups=mesh['str'=16,'crs'=8] {'str','crs'}, use_global_device_ids=true, to_apply=%region_13.15 | all-reduce | flops 4 | bytes 32 | tf_op jit(solution)/shard_map/psum | solution.py:111
  693.3 4.1 scatter_custom_fusion.2
  697.3 147.4 %all-reduce.9.cloned.1.call-done = f32[4,4096]{0,1:T(8,128)} async-done(((f32[4,4096]{0,1:T(8,128)}), f32[4,4096]{0,1:T(8,128)}) %all-reduce.9.cloned.1.call-update) | async-done | bytes 65552 | tf_op jit(solution)/shard_map/psum | solution.py:81
  844.8 10.9 %fusion.56 = f32[4,512]{1,0:T(4,128)S(1)} fusion(f32[4,4096]{0,1:T(8,128)} %all-reduce.9.cloned.1.call-done, f32[512,4096]{1,0:T(8,128)} %param.17), kind=kOutput, calls=%fused_computation.120 | convolution fusion | flops 100663296 | bytes 8462336 | tf_op jit(solution)/shard_map/dot_general | solution.py:82
  855.6 27.8 %all_gather.11 = f32[4,4096]{1,0:T(4,128)S(1)} all-gather(f32[4,512]{1,0:T(4,128)S(1)} %fusion.56), channel_id=1, replica_groups=mesh['str'=16,'crs'=8] {'crs'}, dimensions={1}, use_global_device_ids=true | all-gather | bytes 73728 | tf_op jit(solution)/shard_map/all_gather | solution.py:85
  885.4 3.2 gather_fusion.2
  897.2 70.1 %psum.70 = f32[4]{0:T(128)S(1)} all-reduce(f32[4]{0:T(128)S(1)} %multiply_reduce_fusion.1), channel_id=1, replica_groups=mesh['str'=16,'crs'=8] {'str','crs'}, use_global_device_ids=true, to_apply=%region_18.20 | all-reduce | flops 4 | bytes 32 | tf_op jit(solution)/shard_map/psum | solution.py:93
  972.6 4.0 collective-permute-start.15
  979.9 71.0 %psum.71 = f32[4]{0:T(128)} all-reduce(f32[4]{0:T(128)S(1)} %multiply_reduce_fusion), channel_id=1, replica_groups=mesh['str'=16,'crs'=8] {'str','crs'}, use_global_device_ids=true, to_apply=%region_20.22 | all-reduce | flops 4 | bytes 32 | tf_op jit(solution)/shard_map/psum | solution.py:111
  (184 shorter events, 85.2 us)
Async XLA Ops:
  7.2 181.9 %all-reduce.5.cloned.1.call-start = ((), (), s32[]{:S(2)}) async-start(), calls=%async_computation | async-start | bytes 4194304 | tf_op jit(solution)/shard_map/psum | solution.py:81
  9.5 10.3 collective-permute-start
  11.0 8.6 collective-permute-start.1
  12.4 7.1 collective-permute-start.2
  13.7 5.8 collective-permute-start.3
  30.3 448.3 %all-reduce.7.cloned.1.call-start = ((), (), s32[]{:S(2)}) async-start(), calls=%async_computation.1 | async-start | bytes 4194304 | tf_op jit(solution)/shard_map/psum | solution.py:81
  199.9 30.4 %copy-start.36 = (pred[512]{0:T(512)(128)(4,1)S(1)}, pred[512]{0:T(512)(128)(4,1)}, u32[]{:S(2)}) copy-start(pred[512]{0:T(512)(128)(4,1)} %compare_and_fusion) | copy-start | bytes 1540
  233.2 18.4 %copy-start.18 = (f32[32,2048]{1,0:T(8,128)S(1)}, f32[32,2048]{1,0:T(8,128)}, u32[]{:S(2)}) copy-start(f32[32,2048]{1,0:T(8,128)} %copy-done.17) | copy-start | bytes 786436
  235.8 15.7 %collective-permute-start.4 = (f32[4,1,2048]{2,1,0:T(1,128)S(1)}, f32[4,1,2048]{2,1,0:T(1,128)S(1)}, u32[]{:S(2)}, u32[]{:S(2)}) collective-permute-start(f32[4,1,2048]{2,1,0:T(1,128)S(1)} %get-tuple-element.24), channel_id=1, source_target_pairs={{8,0},{16,8},{24,16},{32,24},{40,32},{48,40},{56,48},{64,56},{72,6... | collective-permute-start | bytes 98312 | tf_op jit(solution)/shard_map/ppermute | solution.py:21
  243.0 8.6 collective-permute-start.5
  244.3 5.4 collective-permute-start.6
  245.6 5.9 collective-permute-start.7
  251.6 70.8 %copy-start.5 = (f32[4,32,2048]{2,1,0:T(8,128)S(1)}, f32[4,32,2048]{2,1,0:T(8,128)}, u32[]{:S(2)}) copy-start(f32[4,32,2048]{2,1,0:T(8,128)} %copy-done.3) | copy-start | bytes 3145732
  330.9 513.9 %all-reduce.9.cloned.1.call-start = ((), (), s32[]{:S(2)}) async-start(), calls=%async_computation.2 | async-start | bytes 4194304 | tf_op jit(solution)/shard_map/psum | solution.py:81
  529.3 71.5 %copy-start.42 = (f32[4]{0:T(128)S(1)}, f32[4]{0:T(128)}, u32[]{:S(2)}) copy-start(f32[4]{0:T(128)} %get-tuple-element.5) | copy-start | bytes 52
  602.8 8.5 collective-permute-start.8
  604.0 7.3 collective-permute-start.9
  604.7 5.7 collective-permute-start.10
  606.0 5.3 collective-permute-start.11
  895.4 72.0 %copy-start.41 = (f32[4]{0:T(128)S(1)}, f32[4]{0:T(128)}, u32[]{:S(2)}) copy-start(f32[4]{0:T(128)} %copy-done.40) | copy-start | bytes 52
  969.4 8.5 collective-permute-start.12
  970.5 7.3 collective-permute-start.13
  971.3 5.7 collective-permute-start.14
  972.6 5.3 collective-permute-start.15
  (38 other events, 224.2 us)
Sparse Core Ops, SparseCore 0:
  30.4 158.5 all-reduce.4
  331.0 147.5 all-reduce.6
  697.5 147.2 all-reduce.8
where the time goes:
time: 1070 us; the launch traced here: 1060 us
  waiting for transfers between devices  458 us (43%)
  blocking collectives  435 us (41%)
  other arithmetic  50.6 us (5%)
  starting transfers between devices  36.5 us (3%)
  local copies, waits for them, and re-layouts  35 us (3%)
  matrix products  32.6 us (3%)
  between operations  14.5 us (1%)
    psum x3, waiting for transfers between devices, coarse_solve(): total = lax.psum(incomplete_value, ('str', 'crs'))  454 us
    psum x3, blocking collectives, precondition(): lax.psum(jnp.sum(remainder * smoothed, axis=(1, 2)), ('str', 'crs'))  209 us
    psum x2, blocking collectives, shards(): lax.psum(jnp.sum(direction * image, axis=(1, 2)), ('str', 'crs'))  142 us
    all_gather x3, blocking collectives, coarse_solve(): correction = lax.all_gather(row_share, 'crs', axis=1, tiled=True)  83.8 us
    dot_general x3, matrix products, coarse_solve(): lax.dot_general(total, coarse_inverse, (((1,), (1,)), ((), ())), precisio...  32.6 us
  transfers between devices with their start and end apart: 19, of which 9 were waited for; matrix products, arithmetic and copies ran while one was open for 0% of the time, Pallas kernels for 0%

commit v1 on v0

--- a/solution.py
+++ b/solution.py
@@ -108,7 +108,9 @@
             - right_link * operate_right_cells
             - left_link * operate_left_cells
         )
-        curvature = lax.psum(jnp.sum(direction * image, axis=(1, 2)), ("str", "crs"))
+        curvature = jnp.sum(direction * image, axis=(1, 2))
+        for mesh_axis in ("crs", "str"):
+            curvature = lax.psum(curvature, mesh_axis)
         alpha = (product / curvature)[:, None, None]
         newton_step = newton_step + alpha * direction
         remainder = remainder - alpha * image

time: 1070 us -> 1090 us (1.019)
    psum x2 -> x6, blocking collectives: 142 us -> 153 us  [shards(): curvature = lax.psum(curvature, mesh_axis)]
where the time goes in v1:
time: 1090 us; the launch traced here: 1070 us
  waiting for transfers between devices  462 us (42%)
  blocking collectives  444 us (41%)
  other arithmetic  50.7 us (5%)
  starting transfers between devices  36.5 us (3%)
  local copies, waits for them, and re-layouts  34.9 us (3%)
  matrix products  32.6 us (3%)
  between operations  14.8 us (1%)
    psum x3, waiting for transfers between devices, coarse_solve(): total = lax.psum(incomplete_value, ('str', 'crs'))  457 us
    psum x3, blocking collectives, precondition(): lax.psum(jnp.sum(remainder * smoothed, axis=(1, 2)), ('str', 'crs'))  207 us
    psum x6, blocking collectives, shards(): curvature = lax.psum(curvature, mesh_axis)  153 us
    all_gather x3, blocking collectives, coarse_solve(): correction = lax.all_gather(row_share, 'crs', axis=1, tiled=True)  84.1 us
    dot_general x3, matrix products, coarse_solve(): lax.dot_general(total, coarse_inverse, (((1,), (1,)), ((), ())), precisio...  32.6 us
  transfers between devices with their start and end apart: 19, of which 9 were waited for; matrix products, arithmetic and copies ran while one was open for 0% of the time, Pallas kernels for 0%

profile of v1, /device:TPU:1, one launch (start us, length us, event | category | flops | bytes accessed | tf_op | source)
XLA Modules:
  0.0 1074.7 jit_solution(3232352265417213428)
XLA Ops:
  13.7 4.2 collective-permute-start.3
  30.4 158.6 %all-reduce.4.cloned.1.call-done = f32[4,4096]{0,1:T(8,128)} async-done(((f32[4,4096]{0,1:T(8,128)}), f32[4,4096]{0,1:T(8,128)}) %all-reduce.4.cloned.1.call-update) | async-done | bytes 65552 | tf_op jit(solution)/shard_map/psum | solution.py:81
  189.0 10.9 %fusion.54 = f32[4,512]{1,0:T(4,128)S(1)} fusion(f32[4,4096]{0,1:T(8,128)} %all-reduce.4.cloned.1.call-done, f32[512,4096]{1,0:T(8,128)} %param.17), kind=kOutput, calls=%fused_computation.118 | convolution fusion | flops 100663296 | bytes 8462336 | tf_op jit(solution)/shard_map/dot_general | solution.py:82
  199.9 28.5 %all_gather.9 = f32[4,4096]{1,0:T(4,128)S(1)} all-gather(f32[4,512]{1,0:T(4,128)S(1)} %fusion.54), channel_id=1, replica_groups=mesh['str'=16,'crs'=8] {'crs'}, dimensions={1}, use_global_device_ids=true | all-gather | bytes 73728 | tf_op jit(solution)/shard_map/all_gather | solution.py:85
  236.1 7.2 collective-permute-start.4
  246.0 4.0 collective-permute-start.7
  252.8 18.1 %psum.86 = f32[4]{0:T(128)} all-reduce(f32[4]{0:T(128)S(1)} %get-tuple-element.3), channel_id=1, replica_groups=mesh['str'=16,'crs'=8] {'crs'}, use_global_device_ids=true, to_apply=%region_6.8 | all-reduce | flops 4 | bytes 32 | tf_op jit(solution)/shard_map/psum | solution.py:113
  271.0 31.5 %psum.87 = f32[4]{0:T(128)} all-reduce(f32[4]{0:T(128)} %psum.86), channel_id=1, replica_groups=mesh['str'=16,'crs'=8] {'str'}, use_global_device_ids=true, to_apply=%region_7.9 | all-reduce | flops 4 | bytes 32 | tf_op jit(solution)/shard_map/psum | solution.py:113
  302.5 66.9 %psum.85 = f32[4]{0:T(128)S(1)} all-reduce(f32[4]{0:T(128)S(1)} %get-tuple-element.4), channel_id=1, replica_groups=mesh['str'=16,'crs'=8] {'str','crs'}, use_global_device_ids=true, to_apply=%region_4.6 | all-reduce | flops 4 | bytes 32 | tf_op jit(solution)/shard_map/psum | solution.py:93
  378.7 147.8 %all-reduce.6.cloned.1.call-done = f32[4,4096]{0,1:T(8,128)} async-done(((f32[4,4096]{0,1:T(8,128)}), f32[4,4096]{0,1:T(8,128)}) %all-reduce.6.cloned.1.call-update) | async-done | bytes 65552 | tf_op jit(solution)/shard_map/psum | solution.py:81
  526.5 10.9 %fusion.55 = f32[4,512]{1,0:T(4,128)S(1)} fusion(f32[4,4096]{0,1:T(8,128)} %all-reduce.6.cloned.1.call-done, f32[512,4096]{1,0:T(8,128)} %param.17), kind=kOutput, calls=%fused_computation.119 | convolution fusion | flops 100663296 | bytes 8462336 | tf_op jit(solution)/shard_map/dot_general | solution.py:82
  537.3 27.8 %all_gather.10 = f32[4,4096]{1,0:T(4,128)S(1)} all-gather(f32[4,512]{1,0:T(4,128)S(1)} %fusion.55), channel_id=1, replica_groups=mesh['str'=16,'crs'=8] {'crs'}, dimensions={1}, use_global_device_ids=true | all-gather | bytes 73728 | tf_op jit(solution)/shard_map/all_gather | solution.py:85
  578.7 69.9 %psum.89 = f32[4]{0:T(128)S(1)} all-reduce(f32[4]{0:T(128)S(1)} %multiply_reduce_fusion.3), channel_id=1, replica_groups=mesh['str'=16,'crs'=8] {'str','crs'}, use_global_device_ids=true, to_apply=%region_12.14 | all-reduce | flops 4 | bytes 32 | tf_op jit(solution)/shard_map/psum | solution.py:93
  653.9 4.0 collective-permute-start.11
  661.2 18.7 %psum.90 = f32[4]{0:T(128)} all-reduce(f32[4]{0:T(128)S(1)} %multiply_reduce_fusion.2), channel_id=1, replica_groups=mesh['str'=16,'crs'=8] {'crs'}, use_global_device_ids=true, to_apply=%region_14.16 | all-reduce | flops 4 | bytes 32 | tf_op jit(solution)/shard_map/psum | solution.py:113
  679.9 32.9 %psum.91 = f32[4]{0:T(128)} all-reduce(f32[4]{0:T(128)} %psum.90), channel_id=1, replica_groups=mesh['str'=16,'crs'=8] {'str'}, use_global_device_ids=true, to_apply=%region_15.17 | all-reduce | flops 4 | bytes 32 | tf_op jit(solution)/shard_map/psum | solution.py:113
  721.4 4.1 scatter_custom_fusion.2
  725.5 150.6 %all-reduce.8.cloned.1.call-done = f32[4,4096]{0,1:T(8,128)} async-done(((f32[4,4096]{0,1:T(8,128)}), f32[4,4096]{0,1:T(8,128)}) %all-reduce.8.cloned.1.call-update) | async-done | bytes 65552 | tf_op jit(solution)/shard_map/psum | solution.py:81
  876.1 10.9 %fusion.56 = f32[4,512]{1,0:T(4,128)S(1)} fusion(f32[4,4096]{0,1:T(8,128)} %all-reduce.8.cloned.1.call-done, f32[512,4096]{1,0:T(8,128)} %param.17), kind=kOutput, calls=%fused_computation.120 | convolution fusion | flops 100663296 | bytes 8462336 | tf_op jit(solution)/shard_map/dot_general | solution.py:82
  886.9 27.8 %all_gather.11 = f32[4,4096]{1,0:T(4,128)S(1)} all-gather(f32[4,512]{1,0:T(4,128)S(1)} %fusion.56), channel_id=1, replica_groups=mesh['str'=16,'crs'=8] {'crs'}, dimensions={1}, use_global_device_ids=true | all-gather | bytes 73728 | tf_op jit(solution)/shard_map/all_gather | solution.py:85
  928.5 70.2 %psum.93 = f32[4]{0:T(128)S(1)} all-reduce(f32[4]{0:T(128)S(1)} %multiply_reduce_fusion.1), channel_id=1, replica_groups=mesh['str'=16,'crs'=8] {'str','crs'}, use_global_device_ids=true, to_apply=%region_20.22 | all-reduce | flops 4 | bytes 32 | tf_op jit(solution)/shard_map/psum | solution.py:93
  1003.9 4.0 collective-permute-start.15
  1011.3 18.7 %psum.94 = f32[4]{0:T(128)} all-reduce(f32[4]{0:T(128)S(1)} %multiply_reduce_fusion), channel_id=1, replica_groups=mesh['str'=16,'crs'=8] {'crs'}, use_global_device_ids=true, to_apply=%region_22.24 | all-reduce | flops 4 | bytes 32 | tf_op jit(solution)/shard_map/psum | solution.py:113
  1030.0 32.7 %psum.95 = f32[4]{0:T(128)} all-reduce(f32[4]{0:T(128)} %psum.94), channel_id=1, replica_groups=mesh['str'=16,'crs'=8] {'str'}, use_global_device_ids=true, to_apply=%region_23.25 | all-reduce | flops 4 | bytes 32 | tf_op jit(solution)/shard_map/psum | solution.py:113
  (186 shorter events, 99.3 us)
Async XLA Ops:
  7.2 181.8 %all-reduce.4.cloned.1.call-start = ((), (), s32[]{:S(2)}) async-start(), calls=%async_computation | async-start | bytes 4194304 | tf_op jit(solution)/shard_map/psum | solution.py:81
  9.5 10.4 collective-permute-start
  11.0 8.7 collective-permute-start.1
  12.4 7.2 collective-permute-start.2
  13.7 5.9 collective-permute-start.3
  30.3 496.1 %all-reduce.6.cloned.1.call-start = ((), (), s32[]{:S(2)}) async-start(), calls=%async_computation.1 | async-start | bytes 4194304 | tf_op jit(solution)/shard_map/psum | solution.py:81
  199.9 30.8 %copy-start.36 = (pred[512]{0:T(512)(128)(4,1)S(1)}, pred[512]{0:T(512)(128)(4,1)}, u32[]{:S(2)}) copy-start(pred[512]{0:T(512)(128)(4,1)} %compare_and_fusion) | copy-start | bytes 1540
  233.5 18.4 %copy-start.13 = (f32[32,2048]{1,0:T(8,128)S(1)}, f32[32,2048]{1,0:T(8,128)}, u32[]{:S(2)}) copy-start(f32[32,2048]{1,0:T(8,128)} %copy-done.12) | copy-start | bytes 786436
  233.5 18.4 %copy-start.18 = (f32[32,2048]{1,0:T(8,128)S(1)}, f32[32,2048]{1,0:T(8,128)}, u32[]{:S(2)}) copy-start(f32[32,2048]{1,0:T(8,128)} %copy-done.17) | copy-start | bytes 786436
  236.1 15.7 %collective-permute-start.4 = (f32[4,1,2048]{2,1,0:T(1,128)S(1)}, f32[4,1,2048]{2,1,0:T(1,128)S(1)}, u32[]{:S(2)}, u32[]{:S(2)}) collective-permute-start(f32[4,1,2048]{2,1,0:T(1,128)S(1)} %get-tuple-element.22), channel_id=1, source_target_pairs={{8,0},{16,8},{24,16},{32,24},{40,32},{48,40},{56,48},{64,56},{72,6... | collective-permute-start | bytes 98312 | tf_op jit(solution)/shard_map/ppermute | solution.py:21
  243.3 8.6 collective-permute-start.5
  244.7 5.4 collective-permute-start.6
  246.0 5.9 collective-permute-start.7
  251.9 118.1 %copy-start.5 = (f32[4,32,2048]{2,1,0:T(8,128)S(1)}, f32[4,32,2048]{2,1,0:T(8,128)}, u32[]{:S(2)}) copy-start(f32[4,32,2048]{2,1,0:T(8,128)} %copy-done.3) | copy-start | bytes 3145732
  378.5 497.6 %all-reduce.8.cloned.1.call-start = ((), (), s32[]{:S(2)}) async-start(), calls=%async_computation.2 | async-start | bytes 4194304 | tf_op jit(solution)/shard_map/psum | solution.py:81
  650.7 8.5 collective-permute-start.8
  651.9 7.3 collective-permute-start.9
  652.6 5.7 collective-permute-start.10
  653.9 5.3 collective-permute-start.11
  926.7 72.1 %copy-start.41 = (f32[4]{0:T(128)S(1)}, f32[4]{0:T(128)}, u32[]{:S(2)}) copy-start(f32[4]{0:T(128)} %copy-done.40) | copy-start | bytes 52
  1000.8 8.5 collective-permute-start.12
  1001.9 7.3 collective-permute-start.13
  1002.7 5.7 collective-permute-start.14
  1003.9 5.3 collective-permute-start.15
  (37 other events, 205.6 us)
Sparse Core Ops, SparseCore 0:
  30.5 158.5 all-reduce.3
  378.6 147.8 all-reduce.5
  725.6 150.4 all-reduce.7
